TPU v7x, 32 devices: a whole 2x2x4 slice. The times are simulated.
32 devices in a mesh: lrow: 2 (over x), rcol: 4 (over y, core), term: 4 (over z).
Axes of the slice: x: 2, y: 2, z: 4, core: 2. Of those that a mesh axis runs over, the one named last changes fastest.
Arguments:
- core_left: bfloat16 [256, 256, 128], P(None, 'rcol'), may hold values from -6 to 6
- core_right: bfloat16 [256, 256, 128], P('rcol', 'lrow'), may hold values from -0.03125 to 0.03125
- env_left: bfloat16 [20, 8, 256], P('term', 'lrow'), may hold values from -0.375 to 0.375
- env_right: bfloat16 [20, 256, 256], P('term'), may hold values from -0.375 to 0.375
- coef_left: float32 [20, 3, 128], P('term'), may hold values from -1.5 to 1.5
- coef_right: float32 [20, 3, 128], P('term'), may hold values from -1.5 to 1.5
- projected: bfloat16 [128, 8, 256, 128], P('term', 'lrow', 'rcol'), may hold values from -6 to 6
Outputs:
- residual: bfloat16 [128, 8, 256, 128], P('term', 'lrow', 'rcol')
All inputs are finite; a program needn't handle non-finite values.
Results may differ from a plain program's by a relative error of at most 0.012.
Values may be sent and summed in bfloat16 or wider, within the bound.
A program may use at most 128 MiB of HBM per device.

v0:
```python
import jax
import jax.numpy as jnp
from jax import lax
from jax.sharding import PartitionSpec as P


def stencil_terms(field, coef):
    wide = field.astype(jnp.float32)
    zero = jnp.zeros_like(wide[..., :1])
    before = jnp.concatenate([zero, wide[..., :-1]], axis=-1)
    after = jnp.concatenate([wide[..., 1:], zero], axis=-1)
    scaled = coef[:, :, None, None, :]
    return scaled[:, 0] * wide[None] + scaled[:, 1] * before[None] + scaled[:, 2] * after[None]


def on_device(core_left, core_right, env_left, env_right, coef_left, coef_right, projected):
    left_field = stencil_terms(core_left, coef_left).astype(jnp.bfloat16)
    left_frame = jnp.einsum(
        "tpq,tqrs->trps", env_left, left_field, preferred_element_type=jnp.float32
    ).astype(jnp.bfloat16)
    left_frame = lax.all_gather(left_frame, "rcol", axis=1, tiled=True)
    right_block = lax.all_gather(core_right, "lrow", axis=1, tiled=True)
    right_field = stencil_terms(right_block, coef_right).astype(jnp.bfloat16)
    right_frame = jnp.einsum(
        "tbq,trqj->trbj", env_right, right_field, preferred_element_type=jnp.float32
    ).astype(jnp.bfloat16)
    partial_sum = jnp.einsum(
        "trai,trbj->jabi",
        left_frame,
        lax.all_to_all(right_frame, "rcol", split_axis=2, concat_axis=1, tiled=True),
        preferred_element_type=jnp.float32,
    )
    summed = lax.psum_scatter(
        partial_sum.astype(jnp.bfloat16), "term", scatter_dimension=0, tiled=True
    ).astype(jnp.float32)
    return (projected.astype(jnp.float32) - summed).astype(jnp.bfloat16)


def solution(mesh):
    return jax.shard_map(
        on_device,
        mesh=mesh,
        in_specs=(
            P(None, "rcol", None),
            P("rcol", "lrow", None),
            P("term", "lrow", None),
            P("term", None, None),
            P("term", None, None),
            P("term", None, None),
            P("term", "lrow", "rcol", None),
        ),
        out_specs=P("term", "lrow", "rcol", None),
        check_vma=False,
    )
```

profile of v0, /device:TPU:0, one launch (start us, length us, event | category | flops | bytes accessed | tf_op | source)
XLA Modules:
  0.0 616.3 jit_solution(12150798259453975703)
XLA Ops:
  7.4 0.7 all-gather.3.cloned.1.call-update
  8.1 0.8 fusion.24
  8.9 60.3 %all-gather.3.cloned.1.call-done = bf16[64,256,128]{2,1,0:T(8,128)(2,1)} async-done(((bf16[64,128,128]{2,1,0:T(8,128)(2,1)}), bf16[64,256,128]{2,1,0:T(8,128)(2,1)}) %all-gather.3.cloned.1.call-update) | async-done | bytes 4194320 | tf_op jit(solution)/shard_map/all_gather | solution.py:22
  69.2 10.7 %fusion.22 = (f32[64,256,127]{2,1,0:T(8,128)}, f32[64,256,127]{2,1,0:T(8,128)}) fusion(bf16[64,256,128]{2,1,0:T(8,128)(2,1)} %all-gather.3.cloned.1.call-done), kind=kLoop, calls=%fused_computation.29 | loop fusion | bytes 33292288 | tf_op jit(solution)/shard_map/slice | solution.py:10
  79.9 9.2 %copy.48 = f32[64,256,127]{1,2,0:T(8,128)} copy(f32[64,256,127]{2,1,0:T(8,128)} %get-tuple-element.7) | data formatting | bytes 16646144
  89.1 9.2 %copy.49 = f32[64,256,127]{1,2,0:T(8,128)} copy(f32[64,256,127]{2,1,0:T(8,128)} %get-tuple-element.8) | data formatting | bytes 16646144
  98.3 8.1 %concatenate.12.clone = f32[64,256,128]{1,2,0:T(8,128)} pad(f32[64,256,127]{1,2,0:T(8,128)} %copy.48, f32[]{:T(128)} %constant.1.clone.1), padding=0_0x0_0x1_0 | pad | bytes 16711684 | tf_op jit(solution)/shard_map/concatenate | solution.py:10
  106.4 3.9 concatenate.13.clone
  110.3 7.0 %copy.23 = f32[64,256,128]{1,2,0:T(8,128)} copy(bf16[64,256,128]{2,1,0:T(8,128)(2,1)} %all-gather.3.cloned.1.call-done) | data formatting | bytes 12582912 | tf_op jit(solution)/shard_map/convert_element_type | solution.py:8
  117.3 19.1 %convert_bitcast_fusion = bf16[5,64,256,128]{2,3,1,0:T(8,128)(2,1)} fusion(f32[64,256,128]{1,2,0:T(8,128)} %concatenate.13.clone, f32[5,128]{1,0:T(8,128)S(1)} %get-tuple-element.15, f32[64,256,128]{1,2,0:T(8,128)} %concatenate.12.clone, f32[5,128]{1,0:T(8,128)S(1)} %get-tuple-element.16, f32[64,256,128]{1,2,0:T(8,128)} %copy.23, f32[5,128]{1,0:T(8,128)S(1)} %bitcast.49, ...), kind=kOutput, calls=%fused_computation.5 | convolution fusion | flops 5442109440 | bytes 46800384 | tf_op jit(solution)/shard_map/tbq,trqj->trbj/dot_general | solution.py:24
  136.4 28.1 %copy.26 = bf16[5,64,256,128]{3,1,0,2:T(8,128)(2,1)} copy(bf16[5,64,256,128]{2,3,1,0:T(8,128)(2,1)} %convert_bitcast_fusion) | data formatting | bytes 41943040 | tf_op jit(solution)/shard_map/convert_element_type | solution.py:26
  164.5 7.9 %all-to-all-start = ((bf16[5,64,256,128]{3,1,0,2:T(8,128)(2,1)}), bf16[5,64,256,128]{3,1,0,2:T(8,128)(2,1)}, u32[]{:S(2)}, u32[]{:S(2)}) async-start(bf16[5,64,256,128]{3,1,0,2:T(8,128)(2,1)} %copy.26), calls=%async_computation | async-start | bytes 41943040 | tf_op jit(solution)/shard_map/all_to_all | solution.py:30
  172.4 0.2 all-gather.5.cloned.1.call-start
  172.6 0.0 copy-start.2
  172.7 8.0 %copy.29 = f32[256,64,128]{2,0,1:T(8,128)} copy(bf16[256,64,128]{2,1,0:T(8,128)(2,1)} %param.7) | data formatting | bytes 12582912 | tf_op jit(solution)/shard_map/convert_element_type | solution.py:8
  180.7 7.3 %fusion.21 = (f32[256,64,127]{2,1,0:T(8,128)}, f32[256,64,127]{2,1,0:T(8,128)}) fusion(bf16[256,64,128]{2,1,0:T(8,128)(2,1)S(1)} %copy-done.2), kind=kLoop, calls=%fused_computation.28 | loop fusion | bytes 33292288 | tf_op jit(solution)/shard_map/slice | solution.py:10
  188.0 8.2 %copy.50 = f32[256,64,127]{2,0,1:T(8,128)S(1)} copy(f32[256,64,127]{2,1,0:T(8,128)} %get-tuple-element.5) | data formatting | bytes 16646144
  196.2 2.2 concatenate.14.clone
  198.5 11.8 %copy.51 = f32[256,64,127]{2,0,1:T(8,128)} copy(f32[256,64,127]{2,1,0:T(8,128)} %get-tuple-element.6) | data formatting | bytes 16646144
  210.3 7.9 %concatenate.15.clone = f32[256,64,128]{2,0,1:T(8,128)} pad(f32[256,64,127]{2,0,1:T(8,128)} %copy.51, f32[]{:T(128)} %constant.1.clone.1), padding=0_0x0_0x0_1 | pad | bytes 16711684 | tf_op jit(solution)/shard_map/concatenate | solution.py:11
  218.2 12.9 %fusion.18 = bf16[5,64,4,128]{3,2,1,0:T(4,128)(2,1)} fusion(f32[256,64,128]{2,0,1:T(8,128)} %concatenate.15.clone, f32[5,128]{1,0:T(8,128)S(1)} %get-tuple-element.17, f32[256,64,128]{2,0,1:T(8,128)S(1)} %concatenate.14.clone, f32[5,128]{1,0:T(8,128)S(1)} %get-tuple-element.18, f32[256,64,128]{2,0,1:T(8,128)S(1)} %bitcast.47, f32[5,128]{1,0:T(8,128)S(1)} %bitcast.50, ...), kind=kOutput, calls=%fused_computation.19 | convolution fusion | flops 146964480 | bytes 25511424 | tf_op jit(solution)/shard_map/tpq,tqrs->trps/dot_general | solution.py:18
  231.0 0.0 all-gather.5.cloned.1.call-update
  231.0 0.0 reduce-scatter.2.cloned.1.call-start
  231.1 176.3 %all-to-all-done = bf16[5,64,256,128]{3,1,0,2:T(8,128)(2,1)} async-done(((bf16[5,64,256,128]{3,1,0,2:T(8,128)(2,1)}), bf16[5,64,256,128]{3,1,0,2:T(8,128)(2,1)}, u32[]{:S(2)}, u32[]{:S(2)}) %all-to-all-start) | async-done | bytes 20971552 | tf_op jit(solution)/shard_map/all_to_all | solution.py:30
  407.4 22.8 %copy.28 = bf16[5,4,64,64,128]{4,3,2,1,0:T(8,128)(2,1)} copy(bf16[5,4,64,64,128]{4,2,0,3,1:T(8,128)(2,1)} %bitcast.6) | data formatting | bytes 41943040 | tf_op jit(solution)/shard_map/all_to_all | solution.py:30
  430.2 28.7 %fusion.12 = bf16[128,4,64,128]{3,0,1,2:T(8,128)(2,1)} fusion(bf16[5,256,64,128,1]{3,2,1,0,4:T(8,128)(2,1)} %bitcast.48, bf16[5,256,4,128]{3,2,1,0:T(4,128)(2,1)} %all-gather.5.cloned.1.call-done), kind=kOutput, calls=%fused_computation.14 | convolution fusion | flops 10741612544 | bytes 30670848 | tf_op jit(solution)/shard_map/trai,trbj->jabi/dot_general | solution.py:27
  458.9 0.0 copy-start.4
  458.9 0.0 copy-start.1
  458.9 0.0 reduce-scatter.2.cloned.1.call-update
  458.9 143.7 %reduce-scatter.2.cloned.1.call-done = bf16[32,4,64,128]{3,0,1,2:T(8,128)(2,1)} async-done(((bf16[128,4,64,128]{3,0,1,2:T(8,128)(2,1)}), bf16[32,4,64,128]{3,0,1,2:T(8,128)(2,1)}) %reduce-scatter.2.cloned.1.call-update) | async-done | bytes 2097168 | tf_op jit(solution)/shard_map/reduce_scatter | solution.py:33
  602.6 3.1 subtract_convert_fusion
  605.7 2.7 copy.34
  (23 shorter events, 0.1 us)
Async XLA Ops:
  7.4 109.9 %copy-start = (bf16[5,256,256]{2,1,0:T(8,128)(2,1)S(1)}, bf16[5,256,256]{2,1,0:T(8,128)(2,1)}, u32[]{:S(2)}) copy-start(bf16[5,256,256]{2,1,0:T(8,128)(2,1)} %param.10) | copy-start | bytes 1966084
  7.4 61.8 %all-gather.3.cloned.1.call-start = ((), (), s32[]{:S(2)}) async-start(), calls=%async_computation.2 | async-start | bytes 6291456 | tf_op jit(solution)/shard_map/all_gather | solution.py:22
  98.3 8.1 %copy-start.3 = (f32[64,256,127]{1,2,0:T(8,128)S(1)}, f32[64,256,127]{1,2,0:T(8,128)}, u32[]{:S(2)}) copy-start(f32[64,256,127]{1,2,0:T(8,128)} %copy.49) | copy-start | bytes 24969220
  164.5 8.1 %copy-start.6 = (f32[5,3,128]{2,1,0:T(4,128)S(1)}, f32[5,3,128]{2,1,0:T(4,128)}, u32[]{:S(2)}) copy-start(f32[5,3,128]{2,1,0:T(4,128)} %param.11) | copy-start | bytes 23044
  164.5 242.9 %all-to-all-start = ((bf16[5,64,256,128]{3,1,0,2:T(8,128)(2,1)}), bf16[5,64,256,128]{3,1,0,2:T(8,128)(2,1)}, u32[]{:S(2)}, u32[]{:S(2)}) async-start(bf16[5,64,256,128]{3,1,0,2:T(8,128)(2,1)} %copy.26), calls=%async_computation | async-start | bytes 41943040 | tf_op jit(solution)/shard_map/all_to_all | solution.py:30
  172.4 257.8 %all-gather.5.cloned.1.call-start = ((), (), s32[]{:S(2)}) async-start(), calls=%async_computation.3 | async-start | bytes 1638400 | tf_op jit(solution)/shard_map/all_gather | solution.py:21
  172.6 8.1 %copy-start.2 = (bf16[256,64,128]{2,1,0:T(8,128)(2,1)S(1)}, bf16[256,64,128]{2,1,0:T(8,128)(2,1)}, u32[]{:S(2)}) copy-start(bf16[256,64,128]{2,1,0:T(8,128)(2,1)} %param.7) | copy-start | bytes 12582916
  198.4 19.7 %slice-start = ((s8[8388608]{0:T(1024)(128)(4,1)}), s8[4194304]{0:T(1024)(128)(4,1)S(1)}, s32[]{:S(2)}) async-start(s8[8388608]{0:T(1024)(128)(4,1)} %bitcast.46), calls=%async_computation.5 | async-start | bytes 8388608
  210.3 7.9 %slice-start.1 = ((s8[8388608]{0:T(1024)(128)(4,1)}), s8[4194304]{0:T(1024)(128)(4,1)S(1)}, s32[]{:S(2)}) async-start(s8[8388608]{0:T(1024)(128)(4,1)} %bitcast.46), calls=%async_computation.6 | async-start | bytes 8388608
  210.3 7.9 %copy-start.5 = (bf16[5,4,256]{2,1,0:T(4,128)(2,1)S(1)}, bf16[5,4,256]{2,1,0:T(4,128)(2,1)}, u32[]{:S(2)}) copy-start(bf16[5,4,256]{2,1,0:T(4,128)(2,1)} %param.9) | copy-start | bytes 30724
  231.0 371.5 %reduce-scatter.2.cloned.1.call-start = ((), (), s32[]{:S(2)}) async-start(), calls=%async_computation.4 | async-start | bytes 10485760 | tf_op jit(solution)/shard_map/reduce_scatter | solution.py:33
  458.9 143.7 %copy-start.4 = (bf16[32,4,64,128]{3,2,1,0:T(8,128)(2,1)S(1)}, bf16[32,4,64,128]{3,2,1,0:T(8,128)(2,1)}, u32[]{:S(2)}) copy-start(bf16[32,4,64,128]{3,2,1,0:T(8,128)(2,1)} %param.13) | copy-start | bytes 6291460
  458.9 149.5 %copy-start.1 = (bf16[5,256,256]{2,1,0:T(8,128)(2,1)S(1)}, bf16[5,256,256]{2,1,0:T(8,128)(2,1)}, u32[]{:S(2)}) copy-start(bf16[5,256,256]{2,1,0:T(8,128)(2,1)} %param.10) | copy-start | bytes 1966084
Sparse Core Ops, SparseCore 0:
  9.7 59.4 all-gather.2
Sparse Core Ops, SparseCore 1:
  231.1 25.6 all-gather.4
  459.0 143.5 reduce-scatter.1
where the time goes:
time: 624 us; the launch traced here: 616 us
  waiting for transfers between devices  381 us (61%)
  local copies, waits for them, and re-layouts  148 us (24%)
  matrix products  60.6 us (10%)
  between operations  15.5 us (2%)
  starting transfers between devices  8.14 us (1%)
    all_to_all x1, waiting for transfers between devices, on_device(): lax.all_to_all(right_frame, 'rcol', split_axis=2, concat_axis=1, tiled=True)  176 us
    reduce_scatter x1, waiting for transfers between devices, on_device(): lax.psum_scatter(partial_sum.astype(jnp.bfloat16), 'term', scatter_dimens...  144 us
    all_gather x1, waiting for transfers between devices, on_device(): right_block = lax.all_gather(core_right, 'lrow', axis=1, tiled=True)  60.3 us
    unnamed x26, local copies, waits for them, and re-layouts  38.5 us
    dot_general x1, matrix products, on_device(): jnp.einsum('trai,trbj->jabi', left_frame, lax.all_to_all(right_frame, 'rc...  28.7 us
    convert_element_type x1, local copies, waits for them, and re-layouts, on_device(): right_frame = jnp.einsum('tbq,trqj->trbj', env_right, right_field, prefer...  28.1 us
    all_to_all x1, local copies, waits for them, and re-layouts, on_device(): lax.all_to_all(right_frame, 'rcol', split_axis=2, concat_axis=1, tiled=True)  22.8 us
    dot_general x1, matrix products, on_device(): jnp.einsum('tbq,trqj->trbj', env_right, right_field, preferred_element_ty...  19.1 us
  transfers between devices with their start and end apart: 4, of which 3 were waited for; matrix products, arithmetic and copies ran while one was open for 13% of the time, Pallas kernels for 0%

commit v1 on v0

v1 whole, which is shorter than its diff:
```python
import functools

import jax
import jax.numpy as jnp
from jax import lax
from jax.experimental import pallas as pl
from jax.experimental.pallas import tpu as pltpu
from jax.sharding import PartitionSpec as P

MESH = pl.DeviceIdType.MESH
ANY = pl.BlockSpec(memory_space=pl.ANY)
VMEM = pl.BlockSpec(memory_space=pltpu.VMEM)
CHUNK = 16
BATCH = 8


def exchange_kernel(
    L, C, T, cr, er, el, cf, cl, crg, erg, lfg, cfg,
    elg, el_all, coef_rows, spread, lf, local_sem, cr_send, cr_recv, crp_send, crp_recv,
    lf_send, lf_recv, lfp_send, lfp_recv, z_send, z_recv,
):
    l, c, z = lax.axis_index("lrow"), lax.axis_index("rcol"), lax.axis_index("term")
    partner = c + 1 - 2 * lax.rem(c, 2)
    H = C // 2
    plane = [(dl, dc) for dl in range(L) for dc in range(H) if dl or dc]

    def at(dl, dc):
        return lax.rem(l + dl, L), lax.rem(c + 2 * dc, C)

    def source(dl, dc):
        return lax.rem(l + L - dl, L), lax.rem(c + C - 2 * dc, C)

    def send(src, dst, sems, recvs, k, where):
        copy = pltpu.make_async_remote_copy(
            src_ref=src, dst_ref=dst, send_sem=sems.at[k], recv_sem=recvs.at[k],
            device_id=where, device_id_type=MESH)
        copy.start()
        return copy

    barrier = pltpu.get_barrier_semaphore()
    for dl, dc in plane:
        pl_, pc = at(dl, dc)
        pl.semaphore_signal(barrier, inc=1, device_id={"lrow": pl_, "rcol": pc}, device_id_type=MESH)
    pl.semaphore_signal(barrier, inc=1, device_id={"rcol": partner}, device_id_type=MESH)
    for d in range(1, T):
        pl.semaphore_signal(barrier, inc=1, device_id={"term": lax.rem(z + d, T)}, device_id_type=MESH)
    pl.semaphore_wait(barrier, len(plane) + 1 + T - 1)

    small = []
    for d in range(1, T):
        where = {"term": lax.rem(z + d, T)}
        small.append(send(el, elg.at[z], z_send, z_recv, 3 * d, where))
        small.append(send(cf, cfg.at[z], z_send, z_recv, 3 * d + 1, where))
    own = [
        pltpu.make_async_copy(el, elg.at[z], local_sem.at[0]),
        pltpu.make_async_copy(cf, cfg.at[z], local_sem.at[1]),
        pltpu.make_async_copy(er, erg.at[z], local_sem.at[2]),
        pltpu.make_async_copy(cr, crg.at[:, l, c], local_sem.at[3]),
    ]
    for copy in own:
        copy.start()
    blocks = []
    for k, (dl, dc) in enumerate(plane):
        pl_, pc = at(dl, dc)
        blocks.append(send(cr, crg.at[:, l, c], cr_send, cr_recv, k, {"lrow": pl_, "rcol": pc}))
    to_partner = [send(cr, crg.at[:, l, c], crp_send, crp_recv, len(plane), {"rcol": partner})]
    envs = [send(er, erg.at[z], z_send, z_recv, 3 * d + 2, {"term": lax.rem(z + d, T)}) for d in range(1, T)]

    own[0].wait()
    own[1].wait()
    for copy in small:
        copy.wait()

    terms, slab = lf.shape[0] // T, lf.shape[2] // 128
    per = terms * slab
    lane = lax.broadcasted_iota(jnp.int32, (slab, 128), 1)
    for s in range(T):
        el_all[s * per:(s + 1) * per, :] = elg[s, 0:per, :]
        for t in range(terms):
            at_row = s * per + t * slab
            for k in range(3):
                row = jnp.broadcast_to(cfg[s, t * 6 + k:t * 6 + k + 1, :], (slab, 128))
                if k == 1:
                    row = jnp.where(lane == 0, 0.0, row)
                if k == 2:
                    row = jnp.where(lane == 127, 0.0, row)
                coef_rows[k, at_row:at_row + slab, :] = row
    for r0 in range(0, lf.shape[1], CHUNK):
        frame = jnp.dot(el_all[...].astype(jnp.bfloat16), cl[:, r0 * 128:(r0 + CHUNK) * 128],
                        preferred_element_type=jnp.float32)
        for r in range(CHUNK):
            x = frame[:, r * 128:(r + 1) * 128]
            spread[r] = (coef_rows[0] * x + coef_rows[1] * pltpu.roll(x, 1, 1)
                         + coef_rows[2] * pltpu.roll(x, 127, 1))
        for t in range(T * terms):
            for a in range(slab):
                lf[t, r0:r0 + CHUNK, a * 128:(a + 1) * 128] = spread[:, t * slab + a, :].astype(jnp.bfloat16)

    frames = []
    for dc in range(1, H):
        _, pc = at(0, dc)
        frames.append(send(lf, lfg.at[:, c], lf_send, lf_recv, dc - 1, {"rcol": pc}))
    frames_partner = [send(lf, lfg.at[:, c], lfp_send, lfp_recv, 0, {"rcol": partner})]
    own.append(pltpu.make_async_copy(lf, lfg.at[:, c], local_sem.at[4]))
    own[-1].start()

    for k, (dl, dc) in enumerate(plane):
        blocks[k].wait_recv()
        sl, sc = source(dl, dc)
        to_partner.append(send(crg.at[:, sl, sc], crg.at[:, sl, sc], crp_send, crp_recv, k, {"rcol": partner}))
    for dc in range(1, H):
        frames[dc - 1].wait_recv()
        _, sc = source(0, dc)
        frames_partner.append(send(lfg.at[:, sc], lfg.at[:, sc], lfp_send, lfp_recv, dc, {"rcol": partner}))
    for copy in envs + to_partner + frames_partner:
        copy.wait()
    for copy in blocks + frames:
        copy.wait_send()
    for copy in own[2:]:
        copy.wait()


def residual_kernel(coef, cr, er, lf, proj, out, h, rf):
    g = pl.program_id(0)
    batch, slab, bb = out.shape[0], out.shape[1], out.shape[2]
    rank = cr.shape[2]
    terms = er.shape[0] // bb
    for s in range(batch + 2):
        j = g * batch + s
        block = jnp.concatenate([cr[j, i] for i in range(cr.shape[1])], axis=1)
        h[s % 4] = lax.dot_general(er[...], block, (((1,), (1,)), ((), ())), preferred_element_type=jnp.float32)
        if s < 2:
            continue
        jj = s - 2
        for t in range(terms):
            rows = slice(t * bb, (t + 1) * bb)
            c = [coef[t * 3 + k, g * batch + jj] for k in range(3)]
            field = (c[0] * h[(jj + 1) % 4, rows, :] + c[1] * h[jj % 4, rows, :] + c[2] * h[(jj + 2) % 4, rows, :])
            rf[jj * bb:(jj + 1) * bb, t * rank:(t + 1) * rank] = field.astype(jnp.bfloat16)
    total = jnp.dot(rf[...], lf[...], preferred_element_type=jnp.float32)
    for jj in range(batch):
        for a in range(slab):
            part = total[jj * bb:(jj + 1) * bb, a * 128:(a + 1) * 128]
            out[jj, a] = (proj[jj, a].astype(jnp.float32) - part).astype(jnp.bfloat16)


def on_device(L, C, T, core_left, core_right, env_left, env_right, coef_left, coef_right, projected):
    terms, slab, rank = env_left.shape
    rb, qb, n = core_right.shape
    jb, _, bb, _ = projected.shape
    z, c = lax.axis_index("term"), lax.axis_index("rcol")
    cr = lax.dynamic_slice_in_dim(jnp.pad(core_right, ((0, 0), (0, 0), (1, 1))), z * jb, jb + 2, 2)
    cr = jnp.transpose(cr, (2, 0, 1))
    er = lax.dynamic_slice_in_dim(env_right, c * bb, bb, 1)
    pad = -(terms * slab) % 8
    el = jnp.pad(env_left.astype(jnp.float32).reshape(terms * slab, rank), ((0, pad), (0, 0)))
    cf = jnp.concatenate([coef_left, coef_right], axis=1).reshape(terms * 6, n)
    cf = jnp.pad(cf, ((0, -(terms * 6) % 8), (0, 0)))
    cl = core_left.reshape(rank, rb * n)
    plane = L * C // 2
    dma = pltpu.SemaphoreType.DMA
    bf16, f32 = jnp.bfloat16, jnp.float32
    crg, erg, lfg, cfg = pl.pallas_call(
        functools.partial(exchange_kernel, L, C, T),
        out_shape=(
            jax.ShapeDtypeStruct((jb + 2, L, C, rb, qb), bf16),
            jax.ShapeDtypeStruct((T, terms, bb, rank), bf16),
            jax.ShapeDtypeStruct((T * terms, C, rb, slab * n), bf16),
            jax.ShapeDtypeStruct((T,) + cf.shape, f32),
        ),
        in_specs=[ANY, ANY, VMEM, VMEM, VMEM],
        out_specs=(ANY, ANY, ANY, VMEM),
        scratch_shapes=[
            pltpu.VMEM((T,) + el.shape, f32),
            pltpu.VMEM((T * terms * slab, rank), f32),
            pltpu.VMEM((3, T * terms * slab, n), f32),
            pltpu.VMEM((CHUNK, T * terms * slab, n), f32),
            pltpu.VMEM((T * terms, rb, slab * n), bf16),
            dma((5,)),
            dma((plane,)), dma((plane,)), dma((plane,)), dma((plane,)),
            dma((C // 2,)), dma((C // 2,)), dma((C // 2,)), dma((C // 2,)),
            dma((3 * T,)), dma((3 * T,)),
        ],
        compiler_params=pltpu.CompilerParams(
            collective_id=0, has_side_effects=True, vmem_limit_bytes=40 * 2**20),
    )(cr, er, el, cf, cl)
    coef = cfg[:, :terms * 6].reshape(T * terms, 2, 3, n)[:, 1].reshape(T * terms * 3, n)
    coef = lax.dynamic_slice_in_dim(coef, z * jb, jb, 1)
    whole = lambda *shape: pl.BlockSpec(shape, lambda g: (0,) * len(shape))
    tile = pl.BlockSpec((BATCH, slab, bb, n), lambda g: (g, 0, 0, 0))
    return pl.pallas_call(
        residual_kernel,
        grid=(jb // BATCH,),
        out_shape=jax.ShapeDtypeStruct(projected.shape, bf16),
        in_specs=[
            pl.BlockSpec(memory_space=pltpu.SMEM),
            whole(jb + 2, L, rank, qb),
            whole(T * terms * bb, rank),
            whole(T * terms * rank, slab * n),
            tile,
        ],
        out_specs=tile,
        scratch_shapes=[
            pltpu.VMEM((4, T * terms * bb, rank), f32),
            pltpu.VMEM((BATCH * bb, T * terms * rank), bf16),
        ],
        compiler_params=pltpu.CompilerParams(vmem_limit_bytes=56 * 2**20),
    )(
        coef,
        crg.reshape(jb + 2, L, rank, qb),
        erg.reshape(T * terms * bb, rank),
        lfg.reshape(T * terms * rank, slab * n),
        projected,
    )


def solution(mesh):
    L, C, T = mesh.shape["lrow"], mesh.shape["rcol"], mesh.shape["term"]
    return jax.shard_map(
        functools.partial(on_device, L, C, T),
        mesh=mesh,
        in_specs=(
            P(None, "rcol", None),
            P("rcol", "lrow", None),
            P("term", "lrow", None),
            P("term", None, None),
            P("term", None, None),
            P("term", None, None),
            P("term", "lrow", "rcol", None),
        ),
        out_specs=P("term", "lrow", "rcol", None),
        check_vma=False,
    )
```

time: 624 us -> 108 us (0.17); the launches traced: 616 us -> 108 us
  waiting for transfers between devices: 381 us -> 0 us
  local copies, waits for them, and re-layouts: 148 us -> 18.2 us
  Pallas kernels: 0 us -> 88.6 us
  matrix products: 60.6 us -> 0 us
  between operations: 15.5 us -> 0.09 us
  starting transfers between devices: 8.14 us -> 0 us
    all_to_all x1 -> x0, waiting for transfers between devices: 176 us -> none  [on_device(): lax.all_to_all(right_frame, 'rcol', split_axis=2, concat_axis=1, tiled=True)]
    reduce_scatter x1 -> x0, waiting for transfers between devices: 144 us -> none  [on_device(): lax.psum_scatter(partial_sum.astype(jnp.bfloat16), 'term', scatter_dimens...]
    pallas_call x0 -> x2, Pallas kernels: none -> 88.6 us  [the longest x1 63.1 us: on_device(): pl.pallas_call(functools.partial(exchange_kernel, L, C, T), out_shape=(ja...]
    dot_general x3 -> x0, matrix products: 60.6 us -> none  [the longest x1 28.7 us: on_device(): jnp.einsum('trai,trbj->jabi', left_frame, lax.all_to_all(right_frame, 'rc...]
    all_gather x2 -> x0, waiting for transfers between devices: 60.3 us -> none  [the longest x1 60.3 us: on_device(): right_block = lax.all_gather(core_right, 'lrow', axis=1, tiled=True)]
    convert_element_type x4 -> x0, local copies, waits for them, and re-layouts: 45.8 us -> none  [the longest x1 28.1 us: on_device(): right_frame = jnp.einsum('tbq,trqj->trbj', env_right, right_field, prefer...]
    all_to_all x1 -> x0, local copies, waits for them, and re-layouts: 22.8 us -> none  [on_device(): lax.all_to_all(right_frame, 'rcol', split_axis=2, concat_axis=1, tiled=True)]
    concatenate x4 -> x0, local copies, waits for them, and re-layouts: 22.1 us -> none  [the longest x2 11.8 us: stencil_terms(): after = jnp.concatenate([wide[..., 1:], zero], axis=-1)]
  transfers between devices with their start and end apart: 4 -> 0, of which waited for: 3 -> 0; matrix products, arithmetic and copies ran while one was open for 13% -> 0% of each run, Pallas kernels for 0% -> 0%
where the time goes in v1:
time: 108 us
  Pallas kernels  88.6 us (82%)
  local copies, waits for them, and re-layouts  18.2 us (17%)
    pallas_call x1, Pallas kernels, on_device(): pl.pallas_call(functools.partial(exchange_kernel, L, C, T), out_shape=(ja...  63.1 us
    pallas_call x1, Pallas kernels, on_device(): pl.pallas_call(residual_kernel, grid=(jb // BATCH,), out_shape=jax.ShapeD...  25.5 us
    unnamed x8, local copies, waits for them, and re-layouts  16.6 us

profile of v1, /device:TPU:0, one launch (start us, length us, event | category | flops | bytes accessed | tf_op | source)
XLA Modules:
  0.0 107.6 jit_solution(13902446826535715692)
XLA Ops:
  0.0 0.0 copy-start
  0.0 0.8 reshape.22
  0.8 0.7 pad_maximum_fusion
  1.5 0.0 copy-done
  1.6 3.3 %copy.10 = bf16[64,128,128]{1,0,2:T(8,128)(2,1)S(1)} copy(bf16[64,128,128]{2,1,0:T(8,128)(2,1)} %param.8) | data formatting | bytes 4194304 | tf_op args[1]
  4.9 0.1 fusion.cr
  5.0 10.3 %copy.13 = bf16[32,8,64,128]{3,1,2,0:T(8,128)(2,1)S(1)} copy(bf16[32,8,64,128]{3,2,1,0:T(8,128)(2,1)} %bitcast.15) | data formatting | bytes 8388608
  15.3 63.1 %shard_map.73 = (bf16[34,2,4,64,128]{4,3,2,1,0:T(8,128)(2,1)S(1)}, bf16[4,5,64,256]{3,2,1,0:T(8,128)(2,1)S(1)}, bf16[20,4,64,512]{3,2,1,0:T(8,128)(2,1)}, f32[4,32,128]{2,1,0:T(8,128)S(1)}) custom-call(bf16[34,64,128]{2,1,0:T(8,128)(2,1)S(1)} %fusion.cr, bf16[5,64,256]{2,1,0:T(8,128)(2,1)S(1)} %constant_dynamic-slice_fusion.1.er, ...), custom_call_target="tpu_custom_call" | custom-call | tf_op jit(solution)/shard_map/pallas_call | solution.py:163
  78.4 0.0 copy-start.1
  78.4 2.1 %copy-done.1 = bf16[34,2,4,64,128]{4,3,2,1,0:T(8,128)(2,1)} copy-done((bf16[34,2,4,64,128]{4,3,2,1,0:T(8,128)(2,1)}, bf16[34,2,4,64,128]{4,3,2,1,0:T(8,128)(2,1)S(1)}, u32[]{:S(2)}) %copy-start.1) | copy-done | bytes 4456472
  80.5 0.0 copy-start.2
  80.5 0.8 copy-done.2
  81.4 0.7 constant_dynamic-slice_fusion.coef
  82.1 25.5 %shard_map.74 = bf16[32,4,64,128]{3,2,1,0:T(8,128)(2,1)} custom-call(f32[60,32]{1,0:T(8,128)} %constant_dynamic-slice_fusion.coef, bf16[34,2,256,128]{3,2,1,0:T(8,128)(2,1)} %bitcast.11, bf16[1280,256]{1,0:T(8,128)(2,1)} %bitcast.12, bf16[5120,512]{1,0:T(8,128)(2,1)} %bitcast.14, bf16[32,4,64,128]{3,2,1,0:T(8,128)(2,1)} %proj.1), custom_call_target="tpu_custom_call" | custom-call | tf_op jit(solution)/shard_map/pallas_call | solution.py:191
  (7 shorter events, 0.1 us)
Async XLA Ops:
  0.0 1.6 %copy-start = (bf16[5,256,256]{2,1,0:T(8,128)(2,1)S(1)}, bf16[5,256,256]{2,1,0:T(8,128)(2,1)}, u32[]{:S(2)}) copy-start(bf16[5,256,256]{2,1,0:T(8,128)(2,1)} %param.10) | copy-start | bytes 1966084
  78.4 2.1 %copy-start.1 = (bf16[34,2,4,64,128]{4,3,2,1,0:T(8,128)(2,1)}, bf16[34,2,4,64,128]{4,3,2,1,0:T(8,128)(2,1)S(1)}, u32[]{:S(2)}) copy-start(bf16[34,2,4,64,128]{4,3,2,1,0:T(8,128)(2,1)S(1)} %get-tuple-element.10) | copy-start | bytes 13369348
  80.5 0.8 copy-start.2

commit v2 on v1

v2 whole, which is shorter than its diff:
```python
import functools

import jax
import jax.numpy as jnp
from jax import lax
from jax.experimental import pallas as pl
from jax.experimental.pallas import tpu as pltpu
from jax.sharding import PartitionSpec as P

MESH = pl.DeviceIdType.MESH
VMEM = pl.BlockSpec(memory_space=pltpu.VMEM)
CHUNK = 16
BATCH = 8
PIECES = 5


def exchange_kernel(
    L, C, T, cr, er, el, cfl, cfr, cl, crg, erg, lfg, cfg,
    el_own, elg, clg, el_all, coef_rows, rows, spread, lf, local_sem, cr_send, cr_recv, crp_send, crp_recv,
    lf_send, lf_recv, lfz_send, lfz_recv, lfp_send, lfp_recv, z_send, z_recv,
):
    l, c, z = lax.axis_index("lrow"), lax.axis_index("rcol"), lax.axis_index("term")
    partner = {"rcol": c + 1 - 2 * lax.rem(c, 2)}
    parity = lax.rem(z, 2)
    beside = {"term": z + 1 - 2 * parity}
    H = C // 2
    terms, slab, _ = el.shape
    per = terms * slab

    def send(src, dst, sems, recvs, k, where):
        copy = pltpu.make_async_remote_copy(
            src_ref=src, dst_ref=dst, send_sem=sems.at[k], recv_sem=recvs.at[k],
            device_id=where, device_id_type=MESH)
        copy.start()
        return copy

    def row_peer(d):
        return {"lrow": lax.rem(l + d, L)}

    def col_peer(d):
        return {"rcol": lax.rem(c + 2 * d, C)}

    def term_peer(d):
        return {"term": lax.rem(z + d, T)}

    def row_source(d):
        return lax.rem(l + L - d, L)

    def col_source(d):
        return lax.rem(c + C - 2 * d, C)

    barrier = pltpu.get_barrier_semaphore()
    peers = ([row_peer(d) for d in range(1, L)] + [col_peer(d) for d in range(1, H)]
             + [term_peer(d) for d in range(1, T)] + [partner])
    for peer in peers:
        pl.semaphore_signal(barrier, inc=1, device_id=peer, device_id_type=MESH)
    el_own[0:per, :] = el[...].astype(jnp.float32).reshape(per, el.shape[2])
    pl.semaphore_wait(barrier, len(peers))

    small = []
    for d in range(1, T):
        small.append(send(el_own, elg.at[z], z_send, z_recv, 4 * d, term_peer(d)))
        small.append(send(cfl, clg.at[z], z_send, z_recv, 4 * d + 1, term_peer(d)))
    blocks = {}
    for d in range(1, H):
        blocks[0, d] = send(cr, crg.at[:, l, c], cr_send, cr_recv, d, col_peer(d))
    for d in range(1, L):
        blocks[d, 0] = send(cr, crg.at[:, l, c], cr_send, cr_recv, d * H, row_peer(d))
    sent = []
    for d in range(1, T):
        sent.append(send(cfr, cfg.at[z], z_send, z_recv, 4 * d + 2, term_peer(d)))
        sent.append(send(er, erg.at[z], z_send, z_recv, 4 * d + 3, term_peer(d)))
    sent.append(send(cr, crg.at[:, l, c], crp_send, crp_recv, 0, partner))
    own = [
        pltpu.make_async_copy(el_own, elg.at[z], local_sem.at[0]),
        pltpu.make_async_copy(cfl, clg.at[z], local_sem.at[1]),
        pltpu.make_async_copy(cfr, cfg.at[z], local_sem.at[2]),
        pltpu.make_async_copy(er, erg.at[z], local_sem.at[3]),
        pltpu.make_async_copy(cr, crg.at[:, l, c], local_sem.at[4]),
    ]
    for copy in own:
        copy.start()
    own[0].wait()
    own[1].wait()
    for copy in small:
        copy.wait()

    lane = lax.broadcasted_iota(jnp.int32, (slab, 128), 1)
    for s in range(T):
        el_all[s * per:(s + 1) * per, :] = elg[s, 0:per, :]
        for t in range(terms):
            at_row = s * per + t * slab
            for k in range(3):
                row = jnp.broadcast_to(clg[s, t, k:k + 1, :], (slab, 128))
                if k == 1:
                    row = jnp.where(lane == 0, 0.0, row)
                if k == 2:
                    row = jnp.where(lane == 127, 0.0, row)
                coef_rows[k, at_row:at_row + slab, :] = row

    @pl.loop(0, lf.shape[1] // CHUNK)
    def _(chunk):
        span = pl.ds(pl.multiple_of(chunk * CHUNK, CHUNK), CHUNK)
        rows[...] = cl[:, span, :].astype(jnp.float32)
        env = el_all[...].astype(jnp.bfloat16)
        for r in range(0, CHUNK, 2):
            block = jnp.concatenate([rows[:, r, :], rows[:, r + 1, :]], axis=1).astype(jnp.bfloat16)
            frame = jnp.dot(env, block, preferred_element_type=jnp.float32)
            for s in range(2):
                x = frame[:, s * 128:(s + 1) * 128]
                spread[r + s] = (coef_rows[0] * x + coef_rows[1] * pltpu.roll(x, 1, 1)
                                 + coef_rows[2] * pltpu.roll(x, 127, 1))
        for t in range(T * terms):
            for a in range(slab):
                lf[t, span, a * 128:(a + 1) * 128] = spread[:, t * slab + a, :].astype(jnp.bfloat16)

    step = T * terms // 2 // PIECES
    mine, theirs = parity * (T * terms // 2), (1 - parity) * (T * terms // 2)
    frames = {}
    for p in range(PIECES):
        for d in range(1, H):
            span = pl.ds(mine + p * step, step)
            frames[p, d] = send(lf.at[span], lfg.at[span, c], lf_send, lf_recv, p * H + d, col_peer(d))
    sent.append(send(lf, lfg.at[:, c], lfp_send, lfp_recv, 0, partner))
    own.append(pltpu.make_async_copy(lf, lfg.at[:, c], local_sem.at[5]))
    own[-1].start()

    for d in range(1, H):
        blocks[0, d].wait_recv()
        block = crg.at[:, l, col_source(d)]
        for e in range(1, L):
            blocks[e, d] = send(block, block, cr_send, cr_recv, e * H + d, row_peer(e))
        sent.append(send(block, block, crp_send, crp_recv, d, partner))
    for e in range(1, L):
        blocks[e, 0].wait_recv()
        block = crg.at[:, row_source(e), c]
        sent.append(send(block, block, crp_send, crp_recv, e * H, partner))
    onward = {}
    for p in range(PIECES):
        for d in range(1, H):
            frames[p, d].wait_recv()
            piece = lfg.at[pl.ds(mine + p * step, step), col_source(d)]
            onward[p, d] = send(piece, piece, lfz_send, lfz_recv, p * H + d, beside)
            sent.append(send(piece, piece, lfp_send, lfp_recv, p * H + d, partner))
    for e in range(1, L):
        for d in range(1, H):
            blocks[e, d].wait_recv()
            block = crg.at[:, row_source(e), col_source(d)]
            sent.append(send(block, block, crp_send, crp_recv, e * H + d, partner))
    for p in range(PIECES):
        for d in range(1, H):
            onward[p, d].wait_recv()
            piece = lfg.at[pl.ds(theirs + p * step, step), col_source(d)]
            sent.append(send(piece, piece, lfp_send, lfp_recv, (PIECES + p) * H + d, partner))
    for copy in sent:
        copy.wait()
    for copies in (blocks, frames, onward):
        for copy in copies.values():
            copy.wait_send()
    for copy in own[2:]:
        copy.wait()


def residual_kernel(proj_rows, coef, cr, er, lf, proj, out, h, rf):
    g = pl.program_id(0)
    batch, slab, bb = out.shape[0], out.shape[1], out.shape[2]
    rank = cr.shape[2]
    terms = er.shape[0] // bb
    first = lax.axis_index("term") * proj_rows
    for s in range(batch + 2):
        j = g * batch + s
        block = jnp.concatenate([cr[j, i] for i in range(cr.shape[1])], axis=1)
        h[s % 4] = lax.dot_general(er[...], block, (((1,), (1,)), ((), ())), preferred_element_type=jnp.float32)
        if s < 2:
            continue
        jj = s - 2
        for t in range(terms):
            rows = slice(t * bb, (t + 1) * bb)
            c = [coef[t * 3 + k, first + g * batch + jj] for k in range(3)]
            field = (c[0] * h[(jj + 1) % 4, rows, :] + c[1] * h[jj % 4, rows, :] + c[2] * h[(jj + 2) % 4, rows, :])
            rf[jj * bb:(jj + 1) * bb, t * rank:(t + 1) * rank] = field.astype(jnp.bfloat16)
    total = jnp.dot(rf[...], lf[...], preferred_element_type=jnp.float32)
    for jj in range(batch):
        for a in range(slab):
            part = total[jj * bb:(jj + 1) * bb, a * 128:(a + 1) * 128]
            out[jj, a] = (proj[jj, a].astype(jnp.float32) - part).astype(jnp.bfloat16)


def on_device(L, C, T, core_left, core_right, env_left, env_right, coef_left, coef_right, projected):
    terms, slab, rank = env_left.shape
    rb, qb, n = core_right.shape
    jb, _, bb, _ = projected.shape
    z, c = lax.axis_index("term"), lax.axis_index("rcol")
    cr = lax.dynamic_slice_in_dim(jnp.pad(core_right, ((0, 0), (0, 0), (1, 1))), z * jb, jb + 2, 2)
    cr = jnp.transpose(cr, (2, 0, 1))
    er = lax.dynamic_slice_in_dim(env_right, c * bb, bb, 1)
    plane = L * C // 2
    parts = PIECES * (C // 2)
    dma = pltpu.SemaphoreType.DMA
    bf16, f32 = jnp.bfloat16, jnp.float32
    crg, erg, lfg, cfg = pl.pallas_call(
        functools.partial(exchange_kernel, L, C, T),
        out_shape=(
            jax.ShapeDtypeStruct((jb + 2, L, C, rb, qb), bf16),
            jax.ShapeDtypeStruct((T, terms, bb, rank), bf16),
            jax.ShapeDtypeStruct((T * terms, C, rb, slab * n), bf16),
            jax.ShapeDtypeStruct((T, terms, 3, n), f32),
        ),
        in_specs=[VMEM] * 6,
        out_specs=(VMEM,) * 4,
        scratch_shapes=[
            pltpu.VMEM((-(-terms * slab // 8) * 8, rank), f32),
            pltpu.VMEM((T, -(-terms * slab // 8) * 8, rank), f32),
            pltpu.VMEM((T, terms, 3, n), f32),
            pltpu.VMEM((T * terms * slab, rank), f32),
            pltpu.VMEM((3, T * terms * slab, n), f32),
            pltpu.VMEM((rank, CHUNK, n), f32),
            pltpu.VMEM((CHUNK, T * terms * slab, n), f32),
            pltpu.VMEM((T * terms, rb, slab * n), bf16),
            dma((6,)),
            dma((plane,)), dma((plane,)), dma((plane,)), dma((plane,)),
            dma((parts,)), dma((parts,)), dma((parts,)), dma((parts,)), dma((2 * parts,)), dma((2 * parts,)),
            dma((4 * T,)), dma((4 * T,)),
        ],
        compiler_params=pltpu.CompilerParams(
            collective_id=0, has_side_effects=True, vmem_limit_bytes=30 * 2**20),
    )(cr, er, env_left, coef_left, coef_right, core_left)
    tile = pl.BlockSpec((BATCH, slab, bb, n), lambda g: (g, 0, 0, 0))
    return pl.pallas_call(
        functools.partial(residual_kernel, jb),
        grid=(jb // BATCH,),
        out_shape=jax.ShapeDtypeStruct(projected.shape, bf16),
        in_specs=[pl.BlockSpec(memory_space=pltpu.SMEM), VMEM, VMEM, VMEM, tile],
        out_specs=tile,
        scratch_shapes=[
            pltpu.VMEM((4, T * terms * bb, rank), f32),
            pltpu.VMEM((BATCH * bb, T * terms * rank), bf16),
        ],
        compiler_params=pltpu.CompilerParams(vmem_limit_bytes=30 * 2**20),
    )(
        cfg.reshape(T * terms * 3, n),
        crg.reshape(jb + 2, L, rank, qb),
        erg.reshape(T * terms * bb, rank),
        lfg.reshape(T * terms * rank, slab * n),
        projected,
    )


def solution(mesh):
    L, C, T = mesh.shape["lrow"], mesh.shape["rcol"], mesh.shape["term"]
    return jax.shard_map(
        functools.partial(on_device, L, C, T),
        mesh=mesh,
        in_specs=(
            P(None, "rcol", None),
            P("rcol", "lrow", None),
            P("term", "lrow", None),
            P("term", None, None),
            P("term", None, None),
            P("term", None, None),
            P("term", "lrow", "rcol", None),
        ),
        out_specs=P("term", "lrow", "rcol", None),
        check_vma=False,
    )
```

time: 108 us -> 81.4 us (0.75)
  Pallas kernels: 88.6 us -> 63.7 us
    pallas_call x1, Pallas kernels: 63.1 us -> 41.4 us  [on_device(): pl.pallas_call(functools.partial(exchange_kernel, L, C, T), out_shape=(ja...]
    pallas_call x1, Pallas kernels: 25.5 us -> 22.4 us  [on_device(): pl.pallas_call(functools.partial(residual_kernel, jb), grid=(jb // BATCH,...]
    unnamed x8 -> x23, local copies, waits for them, and re-layouts: 16.6 us -> 16.5 us
where the time goes in v2:
time: 81.4 us; the launch traced here: 81.1 us
  Pallas kernels  63.7 us (78%)
  local copies, waits for them, and re-layouts  17.3 us (21%)
    pallas_call x1, Pallas kernels, on_device(): pl.pallas_call(functools.partial(exchange_kernel, L, C, T), out_shape=(ja...  41.4 us
    pallas_call x1, Pallas kernels, on_device(): pl.pallas_call(functools.partial(residual_kernel, jb), grid=(jb // BATCH,...  22.4 us
    unnamed x23, local copies, waits for them, and re-layouts  16.5 us

profile of v2, /device:TPU:0, one launch (start us, length us, event | category | flops | bytes accessed | tf_op | source)
XLA Modules:
  0.0 81.1 jit_solution(15358975551675474788)
XLA Ops:
  0.0 0.0 copy-start
  0.0 1.1 %copy-done = bf16[5,256,256]{2,1,0:T(8,128)(2,1)S(1)} copy-done((bf16[5,256,256]{2,1,0:T(8,128)(2,1)S(1)}, bf16[5,256,256]{2,1,0:T(8,128)(2,1)}, u32[]{:S(2)}) %copy-start) | copy-done | bytes 655384
  1.1 0.7 constant_dynamic-slice_fusion.er
  1.8 3.3 %copy.9 = bf16[64,128,128]{1,0,2:T(8,128)(2,1)S(1)} copy(bf16[64,128,128]{2,1,0:T(8,128)(2,1)} %param.8) | data formatting | bytes 4194304 | tf_op args[1]
  5.1 0.0 copy-start.7
  5.1 0.0 copy-start.8
  5.1 0.0 copy-start.9
  5.1 0.0 copy-start.10
  5.1 0.1 fusion.cr
  5.2 0.8 copy-done.7
  6.0 0.0 copy-done.8
  6.0 0.0 copy-done.9
  6.0 0.0 copy-done.10
  6.0 0.0 copy-start.5
  6.0 2.2 %copy-done.5 = bf16[256,64,128]{2,1,0:T(8,128)(2,1)S(1)} copy-done((bf16[256,64,128]{2,1,0:T(8,128)(2,1)S(1)}, bf16[256,64,128]{2,1,0:T(8,128)(2,1)}, u32[]{:S(2)}) %copy-start.5) | copy-done | bytes 4194328
  8.2 0.0 copy-start.6
  8.2 41.4 %shard_map.73 = (bf16[34,2,4,64,128]{4,3,2,1,0:T(8,128)(2,1)S(1)}, bf16[4,5,64,256]{3,2,1,0:T(8,128)(2,1)S(1)}, bf16[20,4,64,512]{3,2,1,0:T(8,128)(2,1)S(1)}, f32[4,5,3,128]{3,2,1,0:T(4,128)S(1)}) custom-call(bf16[34,64,128]{2,1,0:T(8,128)(2,1)S(1)} %fusion.cr, bf16[5,64,256]{2,1,0:T(8,128)(2,1)S(1)} %copy-done.7, bf16[5,4,256]{2,1,0:T(4,128)(2,1)S(1)} %copy-done.8, ...), custom_call_target="tpu_custom_call" | custom-call | tf_op jit(solution)/shard_map/pallas_call | solution.py:201
  49.6 0.0 copy-start.1
  49.6 2.3 %copy-done.1 = bf16[20,4,64,512]{3,2,1,0:T(8,128)(2,1)} copy-done((bf16[20,4,64,512]{3,2,1,0:T(8,128)(2,1)}, bf16[20,4,64,512]{3,2,1,0:T(8,128)(2,1)S(1)}, u32[]{:S(2)}) %copy-start.1) | copy-done | bytes 5242904
  51.8 0.0 copy-start.3
  51.8 2.1 %copy-done.3 = bf16[34,2,4,64,128]{4,3,2,1,0:T(8,128)(2,1)} copy-done((bf16[34,2,4,64,128]{4,3,2,1,0:T(8,128)(2,1)}, bf16[34,2,4,64,128]{4,3,2,1,0:T(8,128)(2,1)S(1)}, u32[]{:S(2)}) %copy-start.3) | copy-done | bytes 4456472
  54.0 0.0 copy-done.6
  54.0 0.0 copy-start.2
  54.0 2.5 %copy-done.2 = bf16[20,4,64,512]{3,2,1,0:T(8,128)(2,1)S(1)} copy-done((bf16[20,4,64,512]{3,2,1,0:T(8,128)(2,1)S(1)}, bf16[20,4,64,512]{3,2,1,0:T(8,128)(2,1)}, u32[]{:S(2)}) %copy-start.2) | copy-done | bytes 5242904
  56.5 0.0 copy-start.4
  56.5 2.3 %copy-done.4 = bf16[34,2,4,64,128]{4,3,2,1,0:T(8,128)(2,1)S(1)} copy-done((bf16[34,2,4,64,128]{4,3,2,1,0:T(8,128)(2,1)S(1)}, bf16[34,2,4,64,128]{4,3,2,1,0:T(8,128)(2,1)}, u32[]{:S(2)}) %copy-start.4) | copy-done | bytes 4456472
  58.7 22.4 %shard_map.74 = bf16[32,4,64,128]{3,2,1,0:T(8,128)(2,1)} custom-call(f32[60,128]{1,0:T(8,128)S(1)} %reshape.12.coef, bf16[34,2,256,128]{3,2,1,0:T(8,128)(2,1)S(1)} %bitcast.6, bf16[1280,256]{1,0:T(8,128)(2,1)S(1)} %bitcast.7, bf16[5120,512]{1,0:T(8,128)(2,1)S(1)} %bitcast.5, bf16[32,4,64,128]{3,2,1,0:T(8,128)(2,1)S(1)} %copy-done.6), custom_call_target="tpu_custom_call" | custom-call | tf_op jit(solution)/shard_map/pallas_call | solution.py:229
  (1 shorter events, 0.0 us)
Async XLA Ops:
  0.0 1.1 %copy-start = (bf16[5,256,256]{2,1,0:T(8,128)(2,1)S(1)}, bf16[5,256,256]{2,1,0:T(8,128)(2,1)}, u32[]{:S(2)}) copy-start(bf16[5,256,256]{2,1,0:T(8,128)(2,1)} %param.10) | copy-start | bytes 1966084
  5.1 0.9 %copy-start.7 = (bf16[5,64,256]{2,1,0:T(8,128)(2,1)S(1)}, bf16[5,64,256]{2,1,0:T(8,128)(2,1)}, u32[]{:S(2)}) copy-start(bf16[5,64,256]{2,1,0:T(8,128)(2,1)} %constant_dynamic-slice_fusion.er) | copy-start | bytes 491524
  5.1 0.9 %copy-start.8 = (bf16[5,4,256]{2,1,0:T(4,128)(2,1)S(1)}, bf16[5,4,256]{2,1,0:T(4,128)(2,1)}, u32[]{:S(2)}) copy-start(bf16[5,4,256]{2,1,0:T(4,128)(2,1)} %el.1) | copy-start | bytes 30724
  5.1 0.9 %copy-start.9 = (f32[5,3,128]{2,1,0:T(4,128)S(1)}, f32[5,3,128]{2,1,0:T(4,128)}, u32[]{:S(2)}) copy-start(f32[5,3,128]{2,1,0:T(4,128)} %cfl.1) | copy-start | bytes 23044
  5.1 0.9 %copy-start.10 = (f32[5,3,128]{2,1,0:T(4,128)S(1)}, f32[5,3,128]{2,1,0:T(4,128)}, u32[]{:S(2)}) copy-start(f32[5,3,128]{2,1,0:T(4,128)} %cfr.1) | copy-start | bytes 23044
  6.0 2.2 %copy-start.5 = (bf16[256,64,128]{2,1,0:T(8,128)(2,1)S(1)}, bf16[256,64,128]{2,1,0:T(8,128)(2,1)}, u32[]{:S(2)}) copy-start(bf16[256,64,128]{2,1,0:T(8,128)(2,1)} %cl.1) | copy-start | bytes 12582916
  8.2 45.8 %copy-start.6 = (bf16[32,4,64,128]{3,2,1,0:T(8,128)(2,1)S(1)}, bf16[32,4,64,128]{3,2,1,0:T(8,128)(2,1)}, u32[]{:S(2)}) copy-start(bf16[32,4,64,128]{3,2,1,0:T(8,128)(2,1)} %proj.1) | copy-start | bytes 6291460
  49.6 2.3 %copy-start.1 = (bf16[20,4,64,512]{3,2,1,0:T(8,128)(2,1)}, bf16[20,4,64,512]{3,2,1,0:T(8,128)(2,1)S(1)}, u32[]{:S(2)}) copy-start(bf16[20,4,64,512]{3,2,1,0:T(8,128)(2,1)S(1)} %get-tuple-element.12) | copy-start | bytes 15728644
  51.8 2.1 %copy-start.3 = (bf16[34,2,4,64,128]{4,3,2,1,0:T(8,128)(2,1)}, bf16[34,2,4,64,128]{4,3,2,1,0:T(8,128)(2,1)S(1)}, u32[]{:S(2)}) copy-start(bf16[34,2,4,64,128]{4,3,2,1,0:T(8,128)(2,1)S(1)} %get-tuple-element.10) | copy-start | bytes 13369348
  54.0 2.5 %copy-start.2 = (bf16[20,4,64,512]{3,2,1,0:T(8,128)(2,1)S(1)}, bf16[20,4,64,512]{3,2,1,0:T(8,128)(2,1)}, u32[]{:S(2)}) copy-start(bf16[20,4,64,512]{3,2,1,0:T(8,128)(2,1)} %copy-done.1) | copy-start | bytes 15728644
  56.5 2.3 %copy-start.4 = (bf16[34,2,4,64,128]{4,3,2,1,0:T(8,128)(2,1)S(1)}, bf16[34,2,4,64,128]{4,3,2,1,0:T(8,128)(2,1)}, u32[]{:S(2)}) copy-start(bf16[34,2,4,64,128]{4,3,2,1,0:T(8,128)(2,1)} %copy-done.3) | copy-start | bytes 13369348

commit v3 on v2

--- a/solution.py
+++ b/solution.py
@@ -14,8 +14,8 @@
 PIECES = 5
 
 
-def exchange_kernel(
-    L, C, T, cr, er, el, cfl, cfr, cl, crg, erg, lfg, cfg,
+def fused_kernel(
+    L, C, T, cr, er, el, cfl, cfr, cl, proj, out, crg, erg, lfg, cfg, coef, h, rf,
     el_own, elg, clg, el_all, coef_rows, rows, spread, lf, local_sem, cr_send, cr_recv, crp_send, crp_recv,
     lf_send, lf_recv, lfz_send, lfz_recv, lfp_send, lfp_recv, z_send, z_recv,
 ):
@@ -66,11 +66,11 @@
         blocks[0, d] = send(cr, crg.at[:, l, c], cr_send, cr_recv, d, col_peer(d))
     for d in range(1, L):
         blocks[d, 0] = send(cr, crg.at[:, l, c], cr_send, cr_recv, d * H, row_peer(d))
-    sent = []
+    sent, environments, to_partner = [], [], []
     for d in range(1, T):
-        sent.append(send(cfr, cfg.at[z], z_send, z_recv, 4 * d + 2, term_peer(d)))
-        sent.append(send(er, erg.at[z], z_send, z_recv, 4 * d + 3, term_peer(d)))
-    sent.append(send(cr, crg.at[:, l, c], crp_send, crp_recv, 0, partner))
+        environments.append(send(cfr, cfg.at[z], z_send, z_recv, 4 * d + 2, term_peer(d)))
+        environments.append(send(er, erg.at[z], z_send, z_recv, 4 * d + 3, term_peer(d)))
+    to_partner.append(send(cr, crg.at[:, l, c], crp_send, crp_recv, 0, partner))
     own = [
         pltpu.make_async_copy(el_own, elg.at[z], local_sem.at[0]),
         pltpu.make_async_copy(cfl, clg.at[z], local_sem.at[1]),
@@ -130,11 +130,11 @@
         block = crg.at[:, l, col_source(d)]
         for e in range(1, L):
             blocks[e, d] = send(block, block, cr_send, cr_recv, e * H + d, row_peer(e))
-        sent.append(send(block, block, crp_send, crp_recv, d, partner))
+        to_partner.append(send(block, block, crp_send, crp_recv, d, partner))
     for e in range(1, L):
         blocks[e, 0].wait_recv()
         block = crg.at[:, row_source(e), c]
-        sent.append(send(block, block, crp_send, crp_recv, e * H, partner))
+        to_partner.append(send(block, block, crp_send, crp_recv, e * H, partner))
     onward = {}
     for p in range(PIECES):
         for d in range(1, H):
@@ -146,7 +146,35 @@
         for d in range(1, H):
             blocks[e, d].wait_recv()
             block = crg.at[:, row_source(e), col_source(d)]
-            sent.append(send(block, block, crp_send, crp_recv, e * H + d, partner))
+            to_partner.append(send(block, block, crp_send, crp_recv, e * H + d, partner))
+    for copy in environments + to_partner:
+        copy.wait()
+    for copy in own[2:5]:
+        copy.wait()
+    to_smem = pltpu.make_async_copy(cfg, coef, local_sem.at[6])
+    to_smem.start()
+    to_smem.wait()
+
+    rank, bb = er.shape[2], er.shape[1]
+    count = T * terms
+    first = z * out.shape[0]
+
+    @pl.loop(0, out.shape[0] // BATCH)
+    def _(g):
+        env = erg[...].reshape(count * bb, rank)
+        for s in range(BATCH + 2):
+            block = jnp.concatenate([crg[g * BATCH + s, i].reshape(rank, cr.shape[2]) for i in range(L)], axis=1)
+            h[s % 4] = lax.dot_general(env, block, (((1,), (1,)), ((), ())), preferred_element_type=jnp.float32)
+            if s < 2:
+                continue
+            jj = s - 2
+            at_row = pl.multiple_of((g * BATCH + jj) * bb, bb)
+            for t in range(count):
+                span = slice(t * bb, (t + 1) * bb)
+                k = [coef[t // terms, t % terms, i, first + g * BATCH + jj] for i in range(3)]
+                field = k[0] * h[(jj + 1) % 4, span, :] + k[1] * h[jj % 4, span, :] + k[2] * h[(jj + 2) % 4, span, :]
+                rf[pl.ds(at_row, bb), t * rank:(t + 1) * rank] = field.astype(jnp.bfloat16)
+
     for p in range(PIECES):
         for d in range(1, H):
             onward[p, d].wait_recv()
@@ -157,33 +185,18 @@
     for copies in (blocks, frames, onward):
         for copy in copies.values():
             copy.wait_send()
-    for copy in own[2:]:
-        copy.wait()
-
-
-def residual_kernel(proj_rows, coef, cr, er, lf, proj, out, h, rf):
-    g = pl.program_id(0)
-    batch, slab, bb = out.shape[0], out.shape[1], out.shape[2]
-    rank = cr.shape[2]
-    terms = er.shape[0] // bb
-    first = lax.axis_index("term") * proj_rows
-    for s in range(batch + 2):
-        j = g * batch + s
-        block = jnp.concatenate([cr[j, i] for i in range(cr.shape[1])], axis=1)
-        h[s % 4] = lax.dot_general(er[...], block, (((1,), (1,)), ((), ())), preferred_element_type=jnp.float32)
-        if s < 2:
-            continue
-        jj = s - 2
-        for t in range(terms):
-            rows = slice(t * bb, (t + 1) * bb)
-            c = [coef[t * 3 + k, first + g * batch + jj] for k in range(3)]
-            field = (c[0] * h[(jj + 1) % 4, rows, :] + c[1] * h[jj % 4, rows, :] + c[2] * h[(jj + 2) % 4, rows, :])
-            rf[jj * bb:(jj + 1) * bb, t * rank:(t + 1) * rank] = field.astype(jnp.bfloat16)
-    total = jnp.dot(rf[...], lf[...], preferred_element_type=jnp.float32)
-    for jj in range(batch):
-        for a in range(slab):
-            part = total[jj * bb:(jj + 1) * bb, a * 128:(a + 1) * 128]
-            out[jj, a] = (proj[jj, a].astype(jnp.float32) - part).astype(jnp.bfloat16)
+    own[5].wait()
+
+    @pl.loop(0, out.shape[0] // BATCH)
+    def _(g):
+        at_row = pl.multiple_of(g * BATCH * bb, BATCH * bb)
+        total = jnp.dot(rf[pl.ds(at_row, BATCH * bb), :], lfg[...].reshape(count * rank, slab * 128),
+                        preferred_element_type=jnp.float32)
+        for jj in range(BATCH):
+            for a in range(slab):
+                part = total[jj * bb:(jj + 1) * bb, a * 128:(a + 1) * 128]
+                j = g * BATCH + jj
+                out[j, a] = (proj[j, a].astype(jnp.float32) - part).astype(jnp.bfloat16)
 
 
 def on_device(L, C, T, core_left, core_right, env_left, env_right, coef_left, coef_right, projected):
@@ -198,17 +211,19 @@
     parts = PIECES * (C // 2)
     dma = pltpu.SemaphoreType.DMA
     bf16, f32 = jnp.bfloat16, jnp.float32
-    crg, erg, lfg, cfg = pl.pallas_call(
-        functools.partial(exchange_kernel, L, C, T),
-        out_shape=(
-            jax.ShapeDtypeStruct((jb + 2, L, C, rb, qb), bf16),
-            jax.ShapeDtypeStruct((T, terms, bb, rank), bf16),
-            jax.ShapeDtypeStruct((T * terms, C, rb, slab * n), bf16),
-            jax.ShapeDtypeStruct((T, terms, 3, n), f32),
-        ),
-        in_specs=[VMEM] * 6,
-        out_specs=(VMEM,) * 4,
+    return pl.pallas_call(
+        functools.partial(fused_kernel, L, C, T),
+        out_shape=jax.ShapeDtypeStruct(projected.shape, bf16),
+        in_specs=[VMEM] * 7,
+        out_specs=VMEM,
         scratch_shapes=[
+            pltpu.VMEM((jb + 2, L, C, rb, qb), bf16),
+            pltpu.VMEM((T, terms, bb, rank), bf16),
+            pltpu.VMEM((T * terms, C, rb, slab * n), bf16),
+            pltpu.VMEM((T, terms, 3, n), f32),
+            pltpu.SMEM((T, terms, 3, n), f32),
+            pltpu.VMEM((4, T * terms * bb, rank), f32),
+            pltpu.VMEM((jb * bb, T * terms * rank), bf16),
             pltpu.VMEM((-(-terms * slab // 8) * 8, rank), f32),
             pltpu.VMEM((T, -(-terms * slab // 8) * 8, rank), f32),
             pltpu.VMEM((T, terms, 3, n), f32),
@@ -217,33 +232,14 @@
             pltpu.VMEM((rank, CHUNK, n), f32),
             pltpu.VMEM((CHUNK, T * terms * slab, n), f32),
             pltpu.VMEM((T * terms, rb, slab * n), bf16),
-            dma((6,)),
+            dma((7,)),
             dma((plane,)), dma((plane,)), dma((plane,)), dma((plane,)),
             dma((parts,)), dma((parts,)), dma((parts,)), dma((parts,)), dma((2 * parts,)), dma((2 * parts,)),
             dma((4 * T,)), dma((4 * T,)),
         ],
         compiler_params=pltpu.CompilerParams(
-            collective_id=0, has_side_effects=True, vmem_limit_bytes=30 * 2**20),
-    )(cr, er, env_left, coef_left, coef_right, core_left)
-    tile = pl.BlockSpec((BATCH, slab, bb, n), lambda g: (g, 0, 0, 0))
-    return pl.pallas_call(
-        functools.partial(residual_kernel, jb),
-        grid=(jb // BATCH,),
-        out_shape=jax.ShapeDtypeStruct(projected.shape, bf16),
-        in_specs=[pl.BlockSpec(memory_space=pltpu.SMEM), VMEM, VMEM, VMEM, tile],
-        out_specs=tile,
-        scratch_shapes=[
-            pltpu.VMEM((4, T * terms * bb, rank), f32),
-            pltpu.VMEM((BATCH * bb, T * terms * rank), bf16),
-        ],
-        compiler_params=pltpu.CompilerParams(vmem_limit_bytes=30 * 2**20),
-    )(
-        cfg.reshape(T * terms * 3, n),
-        crg.reshape(jb + 2, L, rank, qb),
-        erg.reshape(T * terms * bb, rank),
-        lfg.reshape(T * terms * rank, slab * n),
-        projected,
-    )
+            collective_id=0, has_side_effects=True, vmem_limit_bytes=60 * 2**20),
+    )(cr, er, env_left, coef_left, coef_right, core_left, projected)
 
 
 def solution(mesh):

time: 81.4 us -> 77.3 us (0.950)
  local copies, waits for them, and re-layouts: 17.3 us -> 9.12 us
  Pallas kernels: 63.7 us -> 67.9 us
    unnamed x23 -> x4, local copies, waits for them, and re-layouts: 16.5 us -> 7.56 us
    pallas_call x2 -> x1, Pallas kernels: 63.7 us -> 67.9 us  [on_device(): pl.pallas_call(functools.partial(fused_kernel, L, C, T), out_shape=jax.Sh...]
where the time goes in v3:
time: 77.3 us; the launch traced here: 77 us
  Pallas kernels  67.9 us (88%)
  local copies, waits for them, and re-layouts  9.12 us (12%)
    pallas_call x1, Pallas kernels, on_device(): pl.pallas_call(functools.partial(fused_kernel, L, C, T), out_shape=jax.Sh...  67.9 us
    unnamed x4, local copies, waits for them, and re-layouts  7.56 us

profile of v3, /device:TPU:0, one launch (start us, length us, event | category | flops | bytes accessed | tf_op | source)
XLA Modules:
  0.0 77.0 jit_solution(10841222435225909933)
XLA Ops:
  0.0 0.0 copy-start
  0.0 1.1 %copy-done = bf16[5,256,256]{2,1,0:T(8,128)(2,1)S(1)} copy-done((bf16[5,256,256]{2,1,0:T(8,128)(2,1)S(1)}, bf16[5,256,256]{2,1,0:T(8,128)(2,1)}, u32[]{:S(2)}) %copy-start) | copy-done | bytes 655384
  1.1 0.7 constant_dynamic-slice_fusion.er
  1.8 3.3 %copy.8 = bf16[64,128,128]{1,0,2:T(8,128)(2,1)S(1)} copy(bf16[64,128,128]{2,1,0:T(8,128)(2,1)} %param.8) | data formatting | bytes 4194304 | tf_op args[1]
  5.1 0.9 %fusion.cr = bf16[34,64,128]{2,1,0:T(8,128)(2,1)} fusion(s32[]{:T(128)S(6)} %select_n.6, bf16[64,128,128]{1,0,2:T(8,128)(2,1)S(1)} %copy.8), kind=kLoop, calls=%fused_computation.1 | loop fusion | bytes 2654212 | tf_op jit(solution)/shard_map/transpose | solution.py:208
  5.9 67.9 %shard_map.73 = bf16[32,4,64,128]{3,2,1,0:T(8,128)(2,1)} custom-call(bf16[34,64,128]{2,1,0:T(8,128)(2,1)} %fusion.cr, bf16[5,64,256]{2,1,0:T(8,128)(2,1)} %constant_dynamic-slice_fusion.er, bf16[5,4,256]{2,1,0:T(4,128)(2,1)} %el.1, f32[5,3,128]{2,1,0:T(4,128)} %cfl.1, f32[5,3,128]{2,1,0:T(4,128)} %cfr.1, bf16[256,64,128]{2,1,0:T(8,128)(2,1)} %cl.1, ...), custom_call_target="tpu_custom_call" | custom-call | tf_op jit(solution)/shard_map/pallas_call | solution.py:214
  73.8 3.2 %copy.10 = bf16[32,4,64,128]{3,2,1,0:T(8,128)(2,1)} copy(bf16[32,4,64,128]{3,2,1,0:T(8,128)(2,1)} %shard_map.73) | data formatting | bytes 4194304
Async XLA Ops:
  0.0 1.1 %copy-start = (bf16[5,256,256]{2,1,0:T(8,128)(2,1)S(1)}, bf16[5,256,256]{2,1,0:T(8,128)(2,1)}, u32[]{:S(2)}) copy-start(bf16[5,256,256]{2,1,0:T(8,128)(2,1)} %param.10) | copy-start | bytes 1966084
